TPU v7x, 512 devices: a whole 4x4x16 slice. The times are simulated.
512 devices in a mesh: dp: 64 (over y, z), mp: 8 (over x, core).
Axes of the slice: x: 4, y: 4, z: 16, core: 2. Of those that a mesh axis runs over, the one named last changes fastest.
Arguments:
- grads: bfloat16 [64, 64, 512, 256], P('dp', None, 'mp'), may hold values from -16 to 16
- momentum: float32 [64, 512, 256], P('dp', 'mp'), may hold values from -24 to 24
- slots: int32 [64], replicated, may hold values from 0 to 63, each once
Outputs:
- updates: bfloat16 [64, 512, 256], P(None, 'mp')
- new_momentum: float32 [64, 512, 256], P('dp', 'mp')
Inputs may be any that keep to these rules, and one draw needn't show every extreme that they name: slots is a permutation; matrix i is owned by index slots[i] of dp.
All inputs are finite; a program needn't handle non-finite values.
Results may differ from a plain program's by a relative error of at most 0.001.
Values may be sent and summed in bfloat16 or wider, within the bound.
A program may use at most 64 MiB of HBM per device.

v0:
```python
import math

import jax
import jax.numpy as jnp
from jax import lax
from jax.sharding import PartitionSpec as P

ITERS = 5


coef_a = 3.4445
coef_b = -4.775
coef_c = 2.0315


def product(left, right, form):
    return jnp.einsum(
        form, left, right, precision=lax.Precision.HIGHEST, preferred_element_type=jnp.float32
    )


def shards(grads, momentum, slots):
    partial_value = grads[0]
    matrix_count = partial_value.shape[0]
    inverse = (
        jnp.zeros((matrix_count,), jnp.int32)
        .at[slots]
        .set(jnp.arange(matrix_count, dtype=jnp.int32))
    )
    ordered = jnp.take(partial_value, inverse, axis=0).astype(jnp.float32)
    owned_sum = lax.psum_scatter(ordered, "dp", scatter_dimension=0, tiled=True)
    new_momentum = 0.95 * momentum + owned_sum
    blended = owned_sum + 0.95 * new_momentum
    shard_rows = blended.shape[1]
    whole_height = shard_rows * lax.axis_size("mp")
    factor = 0.2 * math.sqrt(max(whole_height, blended.shape[2]))
    whole_rows = lax.all_gather(blended, "mp", axis=1, tiled=True)
    squares = jnp.sum(whole_rows * whole_rows, axis=(1, 2))
    iterate = whole_rows / (jnp.sqrt(squares) + 1e-07)[:, None, None]
    for iteration in range(ITERS):
        gram_matrix = product(iterate, iterate, "mrc,mrd->mcd")
        polynomial = coef_b * gram_matrix + coef_c * product(
            gram_matrix, gram_matrix, "mce,med->mcd"
        )
        iterate = coef_a * iterate + product(iterate, polynomial, "mrc,mcd->mrd")
    first_row = lax.axis_index("mp") * shard_rows
    finals = lax.dynamic_slice_in_dim(iterate, first_row, shard_rows, 1)
    owned_updates = (factor * finals).astype(jnp.bfloat16)
    slot_updates = lax.all_gather(owned_updates, "dp", axis=0, tiled=True)
    updates = jnp.take(slot_updates, slots, axis=0)
    return (updates, new_momentum)


def solution(mesh):
    in_specs = (P("dp", None, "mp", None), P("dp", "mp", None), P())
    out_specs = (P(None, "mp", None), P("dp", "mp", None))
    return jax.shard_map(shards, mesh=mesh, in_specs=in_specs, out_specs=out_specs, check_vma=False)
```

profile of v0, /device:TPU:1, one launch (start us, length us, event | category | flops | bytes accessed | tf_op | source)
XLA Modules:
  0.0 890.2 jit_solution(17898534319144384180)
XLA Ops:
  7.2 0.0 copy-start
  7.2 0.0 reduce-scatter.2.cloned.1.call-start
  7.2 0.8 compare_select_fusion
  8.0 0.8 scatter_custom_fusion
  8.8 0.0 copy-done
  8.9 2.0 gather_fusion
  10.9 3.9 select_convert_fusion
  14.7 0.0 copy-start.1
  14.7 0.0 reduce-scatter.2.cloned.1.call-update
  14.7 0.0 all-gather.2.cloned.1.call-start
  14.8 694.8 %reduce-scatter.2.cloned.1.call-done = f32[1,64,256]{2,1,0:T(8,128)} async-done(((f32[64,64,256]{2,1,0:T(8,128)}), f32[1,64,256]{2,1,0:T(8,128)}) %reduce-scatter.2.cloned.1.call-update) | async-done | bytes 65552 | tf_op jit(solution)/shard_map/reduce_scatter | solution.py:31
  709.6 0.0 copy-done.1
  709.6 1.5 multiply_add_fusion
  711.1 24.9 %all_gather.6 = f32[1,512,256]{2,1,0:T(8,128)S(1)} all-gather(f32[1,64,256]{2,1,0:T(8,128)S(1)} %get-tuple-element.3), channel_id=1, replica_groups=mesh['dp'=64,'mp'=8] {'mp'}, dimensions={1}, use_global_device_ids=true | all-gather | bytes 589824 | tf_op jit(solution)/shard_map/all_gather | solution.py:37
  736.0 0.7 multiply_reduce_fusion
  737.4 1.0 fusion.22
  738.4 0.4 fusion.8
  738.8 0.6 fusion
  739.4 1.0 fusion.19
  740.5 0.4 fusion.7
  740.9 0.6 fusion.1
  741.5 1.0 fusion.16
  742.5 0.4 fusion.6
  742.9 0.6 fusion.2
  743.5 1.0 fusion.13
  744.5 0.4 fusion.5
  744.9 0.0 copy-start.2
  744.9 0.6 fusion.3
  745.5 1.0 fusion.10
  746.6 0.4 fusion.4
  747.0 0.6 convolution_bitcast_fusion
  747.5 0.6 fusion.25
  748.2 0.0 all-gather.2.cloned.1.call-update
  748.2 0.0 copy-done.2
  748.2 128.4 %all-gather.2.cloned.1.call-done = bf16[64,64,256]{2,1,0:T(8,128)(2,1)} async-done(((bf16[1,64,256]{2,1,0:T(8,128)(2,1)}), bf16[64,64,256]{2,1,0:T(8,128)(2,1)}) %all-gather.2.cloned.1.call-update) | async-done | bytes 2097168 | tf_op jit(solution)/shard_map/all_gather | solution.py:49
  876.6 3.6 gather_fusion.1
  880.2 3.2 broadcast_select_fusion
  (6 shorter events, 0.0 us)
Async XLA Ops:
  7.2 1.7 copy-start
  7.2 702.4 %reduce-scatter.2.cloned.1.call-start = ((), (), s32[]{:S(2)}) async-start(), calls=%async_computation.1 | async-start | bytes 4259840 | tf_op jit(solution)/shard_map/reduce_scatter | solution.py:31
  14.7 694.8 %copy-start.1 = (f32[1,64,256]{2,1,0:T(8,128)S(1)}, f32[1,64,256]{2,1,0:T(8,128)}, u32[]{:S(2)}) copy-start(f32[1,64,256]{2,1,0:T(8,128)} %param.6) | copy-start | bytes 196612
  14.7 861.9 %all-gather.2.cloned.1.call-start = ((), (), s32[]{:S(2)}) async-start(), calls=%async_computation.2 | async-start | bytes 2129920 | tf_op jit(solution)/shard_map/all_gather | solution.py:49
  744.9 3.3 copy-start.2
Sparse Core Ops, SparseCore 0:
  14.9 694.6 reduce-scatter.1
  748.3 128.2 all-gather.1
where the time goes:
time: 898 us; the launch traced here: 890 us
  waiting for transfers between devices  823 us (92%)
  blocking collectives  24.9 us (3%)
  between operations  14.9 us (2%)
  other arithmetic  10.7 us (1%)
  matrix products  10 us (1%)
    reduce_scatter x1, waiting for transfers between devices, shards(): owned_sum = lax.psum_scatter(ordered, 'dp', scatter_dimension=0, tiled=True)  695 us
    all_gather x1, waiting for transfers between devices, shards(): slot_updates = lax.all_gather(owned_updates, 'dp', axis=0, tiled=True)  128 us
    all_gather x1, blocking collectives, shards(): whole_rows = lax.all_gather(blended, 'mp', axis=1, tiled=True)  24.9 us
  transfers between devices with their start and end apart: 2, of which 2 were waited for; matrix products, arithmetic and copies ran while one was open for 0% of the time, Pallas kernels for 0%

commit v1 on v0

v1 whole, which is shorter than its diff:
```python
import functools
import math

import jax
import jax.numpy as jnp
from jax import lax
from jax.experimental import pallas as pl
from jax.experimental.pallas import tpu as pltpu
from jax.sharding import PartitionSpec as P

ITERS = 5
coef_a = 3.4445
coef_b = -4.775
coef_c = 2.0315

MESH = pl.DeviceIdType.MESH
NY, NZ, NMP = 4, 16, 8
F32, BF16 = jnp.float32, jnp.bfloat16


def split(value):
    high = value.astype(BF16)
    return high, (value - high.astype(F32)).astype(BF16)


def dot(left, right):
    return jnp.dot(left, right, preferred_element_type=F32)


def product(left, right):
    return dot(left[0], right[0]) + (dot(left[0], right[1]) + dot(left[1], right[0]))


def kernel(
    inverse, slots, grads, momentum, updates, new_momentum,
    held, y_out, y_in, z_out, z_in, rows, final, ordered,
    load_sem, y_ss, y_rs, z_ss, z_rs, mp_ss, mp_rs, gz_ss, gz_rs, gy_ss, gy_rs, out_sem,
):
    dp, mp = lax.axis_index("dp"), lax.axis_index("mp")
    y, z = dp // NZ, lax.rem(dp, NZ)

    def at(dy, dz):
        return (lax.rem(y + dy + NY, NY) * NZ + lax.rem(z + dz + NZ, NZ), mp)

    def remote(src, dst, ss, rs, device):
        return pltpu.make_async_remote_copy(
            src_ref=src, dst_ref=dst, send_sem=ss, recv_sem=rs, device_id=device, device_id_type=MESH
        )

    load = pltpu.make_async_copy(grads.at[0], held, load_sem)
    load.start()
    barrier = pltpu.get_barrier_semaphore()
    partners = [at(o, 0) for o in range(1, NY)] + [at(0, 1), at(0, -1)]
    partners += [(dp, lax.rem(mp + o, NMP)) for o in range(1, NMP)]
    for partner in partners:
        pl.semaphore_signal(barrier, inc=1, device_id=partner, device_id_type=MESH)
    load.wait()

    def chunk(dy, dz):
        return held[inverse[lax.rem(y + dy, NY) * NZ + lax.rem(z + dz + NZ, NZ)]]

    def y_copy(o, group, first, count):
        return remote(
            y_out.at[o - 1, pl.ds(first, count)], y_in.at[o - 1, pl.ds(first, count)],
            y_ss.at[o - 1, group], y_rs.at[o - 1, group], at(o, 0),
        )

    def y_single(group, first, dz):
        for o in range(1, NY):
            y_out[o - 1, first] = chunk(o, dz)
            y_copy(o, group, first, 1).start()

    def y_pair(j):
        for o in range(1, NY):
            y_out[o - 1, 2 * j - 1] = chunk(o, 8 - j)
            y_out[o - 1, 2 * j] = chunk(o, j - 8)
            y_copy(o, j, 2 * j - 1, 2).start()

    def y_sum(k, dz):
        total = chunk(0, dz).astype(F32)
        for o in range(NY - 1):
            total = total + y_in[o, k].astype(F32)
        return total

    def z_copy(way, t):
        return remote(z_out.at[way, t], z_in.at[way, t], z_ss.at[way, t], z_rs.at[way, t], at(0, 1 - 2 * way))

    pl.semaphore_wait(barrier, len(partners))
    y_single(0, 0, 8)
    y_pair(1)

    y_pair(2)
    for o in range(1, NY):
        y_copy(o, 0, 0, 1).wait_recv()
    z_out[0, 0] = y_sum(0, 8)
    z_copy(0, 0).start()

    def z_step(t, _):
        @pl.when(t < 6)
        def _():
            y_pair(t + 2)

        @pl.when(t == 6)
        def _():
            y_single(8, 15, 0)

        for o in range(1, NY):
            y_copy(o, t, 2 * t - 1, 2).wait_recv()
        right = y_sum(2 * t - 1, 8 - t)
        left = y_sum(2 * t, t - 8)
        z_copy(0, t - 1).wait_recv()
        z_out[0, t] = right + z_in[0, t - 1]
        z_copy(0, t).start()

        @pl.when(t > 1)
        def _():
            z_copy(1, t - 1).wait_recv()
            z_out[1, t] = left + z_in[1, t - 1]

        @pl.when(t == 1)
        def _():
            z_out[1, t] = left

        z_copy(1, t).start()
        return 0

    lax.fori_loop(1, 8, z_step, 0)
    for o in range(1, NY):
        y_copy(o, 8, 15, 1).wait_recv()
    owned = y_sum(15, 0)
    z_copy(0, 7).wait_recv()
    z_copy(1, 7).wait_recv()
    owned = owned + z_in[0, 7] + z_in[1, 7]
    fresh = 0.95 * momentum[...] + owned
    new_momentum[...] = fresh
    rows[mp] = owned + 0.95 * fresh

    def mp_copy(o):
        return remote(rows.at[mp], rows.at[mp], mp_ss.at[o - 1], mp_rs.at[o - 1], (dp, lax.rem(mp + o, NMP)))

    def mp_arrival(o):
        other = lax.rem(mp + NMP - o, NMP)
        return remote(rows.at[other], rows.at[other], mp_ss.at[o - 1], mp_rs.at[o - 1], (dp, lax.rem(mp + o, NMP)))

    for o in range(1, NMP):
        mp_copy(o).start()
    for o in range(1, NMP):
        mp_arrival(o).wait_recv()

    whole = rows[...].reshape(NMP * 64, 256)
    scale = 1.0 / (jnp.sqrt(jnp.sum(whole * whole, keepdims=True)) + 1e-07)
    whole = whole * scale
    iterate = rows[mp] * scale
    gram = product(split(whole.T), split(whole))
    for iteration in range(ITERS):
        pair = split(gram)
        poly = split(coef_b * gram + coef_c * product(pair, pair))
        iterate = coef_a * iterate + product(split(iterate), poly)
        if iteration + 1 < ITERS:
            half = coef_a * gram + product(pair, poly)
            gram = coef_a * half + product(split(half), poly)
    factor = 0.2 * math.sqrt(max(NMP * 64, 256))
    mine = y * NZ + z
    final[mine] = (factor * iterate).astype(BF16)

    def gz_slot(way, t):
        return y * NZ + lax.rem(z + NZ + (2 * way - 1) * t, NZ)

    def gz_copy(way, t):
        slot = gz_slot(way, t)
        return remote(final.at[slot], final.at[slot], gz_ss.at[way, t], gz_rs.at[way, t], at(0, 1 - 2 * way))

    def gz_wait(way, t):
        slot = gz_slot(way, t + 1)
        remote(final.at[slot], final.at[slot], gz_ss.at[way, t], gz_rs.at[way, t], at(0, 1 - 2 * way)).wait_recv()

    def gy_copy(o, slot, dz):
        return remote(final.at[slot], final.at[slot], gy_ss.at[o - 1, dz], gy_rs.at[o - 1, dz], at(o, 0))

    def gy_send(dz):
        for o in range(1, NY):
            gy_copy(o, y * NZ + lax.rem(z + dz, NZ), dz).start()

    gz_copy(0, 0).start()
    gz_copy(1, 0).start()
    gy_send(0)

    def gz_step(t, _):
        gz_wait(0, t)

        @pl.when(t < 7)
        def _():
            gz_copy(0, t + 1).start()

        gy_send(NZ - 1 - t)

        @pl.when(t < 7)
        def _():
            gz_wait(1, t)

            @pl.when(t < 6)
            def _():
                gz_copy(1, t + 1).start()

            gy_send(t + 1)

        return 0

    lax.fori_loop(0, 8, gz_step, 0)

    def gy_wait(dz, _):
        for o in range(1, NY):
            gy_copy(o, lax.rem(y + NY - o, NY) * NZ + lax.rem(z + dz, NZ), dz).wait_recv()
        return 0

    lax.fori_loop(0, NZ, gy_wait, 0)

    part = 16
    stores = []
    for first in range(0, NY * NZ, part):
        def place(i, _):
            ordered[first + i] = final[slots[first + i]]
            return 0

        lax.fori_loop(0, part, place, 0)
        store = pltpu.make_async_copy(
            ordered.at[pl.ds(first, part)], updates.at[pl.ds(first, part)], out_sem.at[first // part]
        )
        store.start()
        stores.append(store)

    for o in range(1, NY):
        y_copy(o, 0, 0, 1).wait_send()
        y_copy(o, 8, 15, 1).wait_send()
    for o in range(1, NMP):
        mp_copy(o).wait_send()

    def sent(t, _):
        for o in range(1, NY):
            y_copy(o, t, 2 * t - 1, 2).wait_send()
        z_copy(0, t).wait_send()
        z_copy(1, t).wait_send()
        gz_copy(0, t).wait_send()
        gz_copy(1, t - 1).wait_send()
        return 0

    lax.fori_loop(1, 8, sent, 0)
    z_copy(0, 0).wait_send()
    gz_copy(0, 0).wait_send()

    def gy_sent(dz, _):
        for o in range(1, NY):
            gy_copy(o, y * NZ + lax.rem(z + dz, NZ), dz).wait_send()
        return 0

    lax.fori_loop(0, NZ, gy_sent, 0)
    for store in stores:
        store.wait()


def shards(grads, momentum, slots):
    count = slots.shape[0]
    inverse = jnp.sum(
        jnp.where(slots[:, None] == jnp.arange(count)[None, :], jnp.arange(count, dtype=jnp.int32)[:, None], 0), axis=0
    )
    vmem = pl.BlockSpec(memory_space=pltpu.VMEM)
    smem = pl.BlockSpec(memory_space=pltpu.SMEM)
    anywhere = pl.BlockSpec(memory_space=pl.ANY)
    dma = pltpu.SemaphoreType.DMA
    updates, new_momentum = pl.pallas_call(
        kernel,
        out_shape=(
            jax.ShapeDtypeStruct((64, 64, 256), BF16),
            jax.ShapeDtypeStruct((64, 256), F32),
        ),
        in_specs=[smem, smem, anywhere, vmem],
        out_specs=(anywhere, vmem),
        scratch_shapes=[
            pltpu.VMEM((64, 64, 256), BF16),
            pltpu.VMEM((3, 16, 64, 256), BF16),
            pltpu.VMEM((3, 16, 64, 256), BF16),
            pltpu.VMEM((2, 8, 64, 256), F32),
            pltpu.VMEM((2, 8, 64, 256), F32),
            pltpu.VMEM((NMP, 64, 256), F32),
            pltpu.VMEM((64, 64, 256), BF16),
            pltpu.VMEM((64, 64, 256), BF16),
            dma, dma((3, 9)), dma((3, 9)), dma((2, 8)), dma((2, 8)), dma((7,)), dma((7,)),
            dma((2, 8)), dma((2, 8)), dma((3, 16)), dma((3, 16)), dma((4,)),
        ],
        compiler_params=pltpu.CompilerParams(
            collective_id=0, has_side_effects=True, vmem_limit_bytes=48 * 2**20
        ),
    )(inverse, slots, grads, momentum[0])
    return updates, new_momentum[None]


def solution(mesh):
    in_specs = (P("dp", None, "mp", None), P("dp", "mp", None), P())
    out_specs = (P(None, "mp", None), P("dp", "mp", None))
    return jax.shard_map(shards, mesh=mesh, in_specs=in_specs, out_specs=out_specs, check_vma=False)
```

time: 898 us -> 96.6 us (0.11)
  waiting for transfers between devices: 823 us -> 0 us
  Pallas kernels: 0 us -> 89.3 us
  blocking collectives: 24.9 us -> 0 us
  between operations: 14.9 us -> 0.65 us
  matrix products: 10 us -> 0 us
  other arithmetic: 10.7 us -> 0.75 us
    reduce_scatter x1 -> x0, waiting for transfers between devices: 695 us -> none  [shards(): owned_sum = lax.psum_scatter(ordered, 'dp', scatter_dimension=0, tiled=True)]
    all_gather x1 -> x0, waiting for transfers between devices: 128 us -> none  [shards(): slot_updates = lax.all_gather(owned_updates, 'dp', axis=0, tiled=True)]
    pallas_call x0 -> x1, Pallas kernels: none -> 89.3 us  [shards(): pl.pallas_call(kernel, out_shape=(jax.ShapeDtypeStruct((64, 64, 256), BF1...]
    all_gather x1 -> x0, blocking collectives: 24.9 us -> none  [shards(): whole_rows = lax.all_gather(blended, 'mp', axis=1, tiled=True)]
    dot_general x15 -> x0, matrix products: 10 us -> none  [product(): jnp.einsum(form, left, right, precision=lax.Precision.HIGHEST, preferred_...]
  transfers between devices with their start and end apart: 2 -> 0, of which waited for: 2 -> 0; matrix products, arithmetic and copies ran while one was open for 0% -> 0% of each run, Pallas kernels for 0% -> 0%
where the time goes in v1:
time: 96.6 us; the launch traced here: 95.7 us
  Pallas kernels  89.3 us (92%)
  local copies, waits for them, and re-layouts  5.03 us (5%)
    pallas_call x1, Pallas kernels, shards(): pl.pallas_call(kernel, out_shape=(jax.ShapeDtypeStruct((64, 64, 256), BF1...  89.3 us
    unnamed x8, local copies, waits for them, and re-layouts  5.03 us

profile of v1, /device:TPU:1, one launch (start us, length us, event | category | flops | bytes accessed | tf_op | source)
XLA Modules:
  0.0 95.7 jit_solution(1289856662891144600)
XLA Ops:
  0.6 0.7 select_reduce_fusion.inverse
  1.4 0.0 copy-start
  1.4 1.6 %copy-done = bf16[1,64,64,256]{3,2,1,0:T(8,128)(2,1)S(1)} copy-done((bf16[1,64,64,256]{3,2,1,0:T(8,128)(2,1)S(1)}, bf16[1,64,64,256]{3,2,1,0:T(8,128)(2,1)}, u32[]{:S(2)}) %copy-start) | copy-done | bytes 2097176
  3.0 0.0 copy-start.1
  3.0 0.8 copy-done.1
  3.8 0.0 copy-start.2
  3.8 0.7 copy-done.2
  4.5 89.3 %shard_map.50 = (bf16[64,64,256]{2,1,0:T(8,128)(2,1)S(1)}, f32[64,256]{1,0:T(8,128)S(1)}) custom-call(s32[64]{0:T(128)S(1)} %select_reduce_fusion.inverse, s32[64]{0:T(128)S(1)} %copy-done.2, bf16[1,64,64,256]{3,2,1,0:T(8,128)(2,1)S(1)} %copy-done, f32[64,256]{1,0:T(8,128)S(1)} %bitcast.2), custom_call_target="tpu_custom_call" | custom-call | tf_op jit(solution)/shard_map/pallas_call | solution.py:270
  93.8 1.3 %copy.7 = bf16[64,64,256]{2,1,0:T(8,128)(2,1)} copy(bf16[64,64,256]{2,1,0:T(8,128)(2,1)S(1)} %get-tuple-element.8) | data formatting | bytes 4194304
  95.1 0.6 copy.8
Async XLA Ops:
  1.4 1.6 %copy-start = (bf16[1,64,64,256]{3,2,1,0:T(8,128)(2,1)S(1)}, bf16[1,64,64,256]{3,2,1,0:T(8,128)(2,1)}, u32[]{:S(2)}) copy-start(bf16[1,64,64,256]{3,2,1,0:T(8,128)(2,1)} %grads.1) | copy-start | bytes 6291460
  3.0 0.8 copy-start.1
  3.8 0.7 copy-start.2

commit v2 on v1

v2 whole, which is shorter than its diff:
```python
import functools
import math

import jax
import jax.numpy as jnp
from jax import lax
from jax.experimental import pallas as pl
from jax.experimental.pallas import tpu as pltpu
from jax.sharding import PartitionSpec as P

ITERS = 5
coef_a = 3.4445
coef_b = -4.775
coef_c = 2.0315

MESH = pl.DeviceIdType.MESH
NY, NZ, NMP = 4, 16, 8
SUM_PARENT = {8: 7, 7: 6, 6: 5, 5: 3, 4: 3, 3: 0, 2: 1, 1: 0}
SUM_ORDER = (8, 7, 6, 4, 5, 2, 3, 1, 0)
SPREAD_PARENT = {8: 7, 7: 5, 6: 5, 5: 3, 4: 3, 3: 0, 2: 1, 1: 0}
SPREAD_ORDER = (
    ("b", 0), ("m", 1), ("m", 3), ("b", 1), ("m", 2), ("b", 3), ("m", 4), ("m", 5), ("b", 2),
    ("b", 4), ("b", 5), ("m", 6), ("m", 7), ("b", 6), ("b", 7), ("m", 8), ("b", 8),
)
AHEAD = 3
HOPS = sorted({d - p for parent in (SUM_PARENT, SPREAD_PARENT) for d, p in parent.items()})
FIRST = 48
F32, BF16 = jnp.float32, jnp.bfloat16


def split(value):
    high = value.astype(BF16)
    return high, (value - high.astype(F32)).astype(BF16)


def dot(left, right):
    return jnp.dot(left, right, preferred_element_type=F32)


def product(left, right):
    return dot(left[0], right[0]) + (dot(left[0], right[1]) + dot(left[1], right[0]))


def kernel(
    table, grads, momentum, updates, new_momentum,
    held, y_out, y_in, z_out, z_in, rows, final, ordered,
    load_sem, y_ss, y_rs, z_ss, z_rs, mp_ss, mp_rs, g_ss, g_rs, gy_ss, gy_rs, out_sem,
):
    dp, mp = lax.axis_index("dp"), lax.axis_index("mp")
    y, z = dp // NZ, lax.rem(dp, NZ)

    def at(dy, dz):
        return (lax.rem(y + dy + NY, NY) * NZ + lax.rem(z + dz + NZ, NZ), mp)

    def remote(src, dst, ss, rs, device):
        return pltpu.make_async_remote_copy(
            src_ref=src, dst_ref=dst, send_sem=ss, recv_sem=rs, device_id=device, device_id_type=MESH
        )

    load = pltpu.make_async_copy(grads.at[0], held, load_sem)
    load.start()
    barrier = pltpu.get_barrier_semaphore()
    partners = [at(o, 0) for o in range(1, NY)] + [at(0, s * k) for k in HOPS for s in (1, -1)]
    partners += [(dp, lax.rem(mp + o, NMP)) for o in range(1, NMP)]
    for partner in partners:
        pl.semaphore_signal(barrier, inc=1, device_id=partner, device_id_type=MESH)

    def ways(d):
        return ((0, 1), (1, -1)) if 0 < d < 8 else ((0, 1),)

    def children(parent, d):
        return [c for c in parent if parent[c] == d]

    position, spots = {}, 0
    for d in SUM_ORDER:
        position[d] = spots
        spots += len(ways(d))

    def chunk(dy, dz):
        return held[table[0, lax.rem(y + dy, NY) * NZ + lax.rem(z + dz + NZ, NZ)]]

    def y_copy(o, d):
        part = pl.ds(position[d], len(ways(d)))
        return remote(y_out.at[o - 1, part], y_in.at[o - 1, part], y_ss.at[o - 1, d], y_rs.at[o - 1, d], at(o, 0))

    def y_send(d):
        for o in range(1, NY):
            for way, sign in ways(d):
                y_out[o - 1, position[d] + way] = chunk(o, sign * d)
            y_copy(o, d).start()

    def z_copy(way, sign, d):
        return remote(
            z_out.at[way, d - 1], z_in.at[way, d - 1], z_ss.at[way, d - 1], z_rs.at[way, d - 1],
            at(0, sign * (d - SUM_PARENT[d])),
        )

    load.wait()
    pl.semaphore_wait(barrier, len(partners))
    for d in SUM_ORDER[:AHEAD]:
        y_send(d)
    for index, d in enumerate(SUM_ORDER):
        if index + AHEAD < len(SUM_ORDER):
            y_send(SUM_ORDER[index + AHEAD])
        for o in range(1, NY):
            y_copy(o, d).wait_recv()
        for way, sign in ways(d):
            total = chunk(0, sign * d).astype(F32)
            for o in range(1, NY):
                total = total + y_in[o - 1, position[d] + way].astype(F32)
            for side, step in ways(d) if d else ways(1):
                if side == way or d == 0:
                    for c in children(SUM_PARENT, d):
                        if c < 8 or side == 0:
                            z_copy(side, step, c).wait_recv()
                            total = total + z_in[side, c - 1]
            if d:
                z_out[way, d - 1] = total
                z_copy(way, sign, d).start()
    fresh = 0.95 * momentum[...] + total
    new_momentum[...] = fresh
    rows[mp] = total + 0.95 * fresh

    def mp_copy(o):
        return remote(rows.at[mp], rows.at[mp], mp_ss.at[o - 1], mp_rs.at[o - 1], (dp, lax.rem(mp + o, NMP)))

    def mp_arrival(o):
        other = lax.rem(mp + NMP - o, NMP)
        return remote(rows.at[other], rows.at[other], mp_ss.at[o - 1], mp_rs.at[o - 1], (dp, lax.rem(mp + o, NMP)))

    for o in range(1, NMP):
        mp_copy(o).start()
    for o in range(1, NMP):
        mp_arrival(o).wait_recv()

    whole = rows[...].reshape(NMP * 64, 256)
    scale = 1.0 / (jnp.sqrt(jnp.sum(whole * whole, keepdims=True)) + 1e-07)
    whole = whole * scale
    iterate = rows[mp] * scale
    gram = product(split(whole.T), split(whole))
    for iteration in range(ITERS):
        pair = split(gram)
        poly = split(coef_b * gram + coef_c * product(pair, pair))
        if iteration + 1 < ITERS:
            both = jnp.concatenate([gram, iterate], axis=0)
            both = coef_a * both + product(split(both), poly)
            half, iterate = both[:256], both[256:]
            gram = coef_a * half + product(split(half), poly)
        else:
            iterate = coef_a * iterate + product(split(iterate), poly)
    factor = 0.2 * math.sqrt(max(NMP * 64, 256))
    final[0, z] = (factor * iterate).astype(BF16)

    first_rows, other_rows = pl.ds(0, FIRST), pl.ds(FIRST, 64 - FIRST)

    def spread(kind, way, sign, d, step):
        source = d if step == 2 else SPREAD_PARENT[d]
        origin = lax.rem(z + NZ - sign * source, NZ)
        part = final.at[0, origin] if kind == "m" else final.at[pl.ds(1, NY - 1), origin, other_rows]
        which = 0 if kind == "m" else 1
        return remote(part, part, g_ss.at[which, way, d - 1], g_rs.at[which, way, d - 1], at(0, sign * (d - SPREAD_PARENT[d])))

    def across(o, sender_z, rows_of, index):
        return remote(
            final.at[0, sender_z, rows_of], final.at[NY - o, sender_z, rows_of],
            gy_ss.at[o - 1, index], gy_rs.at[o - 1, index], at(o, 0),
        )

    def across_arrival(o, sender_z, rows_of, index):
        return remote(
            final.at[0, sender_z, rows_of], final.at[NY - o, sender_z, rows_of],
            gy_ss.at[o - 1, index], gy_rs.at[o - 1, index], at(o, 0),
        )

    def send_on(kind, d):
        for c in sorted(children(SPREAD_PARENT, d), reverse=True):
            for way, sign in ways(d) if d else ways(1):
                if c < 8 or way == 0:
                    spread(kind, way, sign, c, 1).start()

    def send_across(dz, index):
        for o in range(1, NY):
            across(o, lax.rem(z + dz + NZ, NZ), first_rows, index).start()

    for o in range(1, NY):
        across(o, z, other_rows, 16).start()
    send_on("m", 0)
    send_across(0, 0)
    sent = [(0, 0)]
    for kind, d in SPREAD_ORDER:
        if d == 0:
            for o in range(1, NY):
                across_arrival(o, z, other_rows, 16).wait_recv()
            send_on(kind, 0)
            continue
        for way, sign in ways(d):
            spread(kind, way, sign, d, 2).wait_recv()
            for c in children(SPREAD_PARENT, d):
                if c < 8 or way == 0:
                    spread(kind, way, sign, c, 1).start()
            if kind == "m":
                send_across(-sign * d, len(sent))
                sent.append((-sign * d, len(sent)))
    for dz, index in sent:
        for o in range(1, NY):
            across_arrival(o, lax.rem(z + dz + NZ, NZ), first_rows, index).wait_recv()

    part = 16
    stores = []
    for first in range(0, NY * NZ, part):
        def place(i, _):
            slot = table[1, first + i]
            ordered[first + i] = final[lax.rem(slot // NZ + NY - y, NY), lax.rem(slot, NZ)]
            return 0

        lax.fori_loop(0, part, place, 0)
        store = pltpu.make_async_copy(
            ordered.at[pl.ds(first, part)], updates.at[pl.ds(first, part)], out_sem.at[first // part]
        )
        store.start()
        stores.append(store)

    for d in SUM_ORDER:
        for o in range(1, NY):
            y_copy(o, d).wait_send()
        for way, sign in ways(d):
            if d:
                z_copy(way, sign, d).wait_send()
                spread("m", way, sign, d, 1).wait_send()
                spread("b", way, sign, d, 1).wait_send()
    for o in range(1, NMP):
        mp_copy(o).wait_send()
    for dz, index in sent:
        for o in range(1, NY):
            across(o, lax.rem(z + dz + NZ, NZ), first_rows, index).wait_send()
    for o in range(1, NY):
        across(o, z, other_rows, 16).wait_send()
    for store in stores:
        store.wait()


def shards(grads, momentum, slots):
    matrix = lax.broadcasted_iota(jnp.int32, (2, 64, 64), 1)
    column = lax.broadcasted_iota(jnp.int32, (2, 64, 64), 2)
    forward = lax.broadcasted_iota(jnp.int32, (2, 64, 64), 0) == 1
    slot = slots[None, :, None]
    table = jnp.sum(
        jnp.where(forward, jnp.where(matrix == column, slot, 0), jnp.where(slot == column, matrix, 0)), axis=1
    )
    vmem = pl.BlockSpec(memory_space=pltpu.VMEM)
    smem = pl.BlockSpec(memory_space=pltpu.SMEM)
    anywhere = pl.BlockSpec(memory_space=pl.ANY)
    dma = pltpu.SemaphoreType.DMA
    updates, new_momentum = pl.pallas_call(
        kernel,
        out_shape=(
            jax.ShapeDtypeStruct((64, 64, 256), BF16),
            jax.ShapeDtypeStruct((64, 256), F32),
        ),
        in_specs=[smem, anywhere, vmem],
        out_specs=(anywhere, vmem),
        scratch_shapes=[
            pltpu.VMEM((64, 64, 256), BF16),
            pltpu.VMEM((3, 16, 64, 256), BF16),
            pltpu.VMEM((3, 16, 64, 256), BF16),
            pltpu.VMEM((2, 8, 64, 256), F32),
            pltpu.VMEM((2, 8, 64, 256), F32),
            pltpu.VMEM((NMP, 64, 256), F32),
            pltpu.VMEM((NY, NZ, 64, 256), BF16),
            pltpu.VMEM((64, 64, 256), BF16),
            dma, dma((3, 9)), dma((3, 9)), dma((2, 8)), dma((2, 8)), dma((7,)), dma((7,)),
            dma((2, 2, 8)), dma((2, 2, 8)), dma((3, 17)), dma((3, 17)), dma((4,)),
        ],
        compiler_params=pltpu.CompilerParams(
            collective_id=0, has_side_effects=True, vmem_limit_bytes=50 * 2**20
        ),
    )(table, grads, momentum[0])
    return updates, new_momentum[None]


def solution(mesh):
    in_specs = (P("dp", None, "mp", None), P("dp", "mp", None), P())
    out_specs = (P(None, "mp", None), P("dp", "mp", None))
    return jax.shard_map(shards, mesh=mesh, in_specs=in_specs, out_specs=out_specs, check_vma=False)
```

time: 96.6 us -> 85.6 us (0.89)
  Pallas kernels: 89.3 us -> 81.2 us
  local copies, waits for them, and re-layouts: 5.03 us -> 2.79 us
    pallas_call x1, Pallas kernels: 89.3 us -> 81.2 us  [shards(): pl.pallas_call(kernel, out_shape=(jax.ShapeDtypeStruct((64, 64, 256), BF1...]
    unnamed x8 -> x4, local copies, waits for them, and re-layouts: 5.03 us -> 2.79 us
where the time goes in v2:
time: 85.6 us; the launch traced here: 85.4 us
  Pallas kernels  81.2 us (95%)
  local copies, waits for them, and re-layouts  2.79 us (3%)
    pallas_call x1, Pallas kernels, shards(): pl.pallas_call(kernel, out_shape=(jax.ShapeDtypeStruct((64, 64, 256), BF1...  81.2 us
    unnamed x4, local copies, waits for them, and re-layouts  2.79 us

profile of v2, /device:TPU:1, one launch (start us, length us, event | category | flops | bytes accessed | tf_op | source)
XLA Modules:
  0.0 85.4 jit_solution(1910397093494339601)
XLA Ops:
  0.6 0.8 select_reduce_fusion.table
  1.4 0.0 copy-start
  1.4 0.8 copy-done
  2.2 81.2 %shard_map.50 = (bf16[64,64,256]{2,1,0:T(8,128)(2,1)S(1)}, f32[64,256]{1,0:T(8,128)S(1)}) custom-call(s32[2,64]{1,0:T(2,128)S(1)} %select_reduce_fusion.table, bf16[1,64,64,256]{3,2,1,0:T(8,128)(2,1)} %grads.1, f32[64,256]{1,0:T(8,128)S(1)} %bitcast.2), custom_call_target="tpu_custom_call" | custom-call | tf_op jit(solution)/shard_map/pallas_call | solution.py:254
  83.4 1.3 %copy.7 = bf16[64,64,256]{2,1,0:T(8,128)(2,1)} copy(bf16[64,64,256]{2,1,0:T(8,128)(2,1)S(1)} %get-tuple-element.8) | data formatting | bytes 4194304
  84.8 0.6 copy.8
  (1 shorter events, 0.0 us)
Async XLA Ops:
  1.4 0.8 copy-start

commit v3 on v2

--- a/solution.py
+++ b/solution.py
@@ -23,6 +23,7 @@
     ("b", 4), ("b", 5), ("m", 6), ("m", 7), ("b", 6), ("b", 7), ("m", 8), ("b", 8),
 )
 AHEAD = 3
+PIECES = 1
 HOPS = sorted({d - p for parent in (SUM_PARENT, SPREAD_PARENT) for d, p in parent.items()})
 FIRST = 48
 F32, BF16 = jnp.float32, jnp.bfloat16
@@ -43,8 +44,8 @@
 
 def kernel(
     table, grads, momentum, updates, new_momentum,
-    held, y_out, y_in, z_out, z_in, rows, final, ordered,
-    load_sem, y_ss, y_rs, z_ss, z_rs, mp_ss, mp_rs, g_ss, g_rs, gy_ss, gy_rs, out_sem,
+    held, y_out, y_in, z_out, z_in, rows, final,
+    load_sem, y_ss, y_rs, z_ss, z_rs, mp_ss, mp_rs, g_ss, g_rs, gy_ss, gy_rs,
 ):
     dp, mp = lax.axis_index("dp"), lax.axis_index("mp")
     y, z = dp // NZ, lax.rem(dp, NZ)
@@ -61,7 +62,7 @@
     load.start()
     barrier = pltpu.get_barrier_semaphore()
     partners = [at(o, 0) for o in range(1, NY)] + [at(0, s * k) for k in HOPS for s in (1, -1)]
-    partners += [(dp, lax.rem(mp + o, NMP)) for o in range(1, NMP)]
+    partners += [(dp, lax.rem(mp + 2 * o, NMP)) for o in range(1, 4)] + [(dp, mp + 1 - 2 * lax.rem(mp, 2))]
     for partner in partners:
         pl.semaphore_signal(barrier, inc=1, device_id=partner, device_id_type=MESH)
 
@@ -121,17 +122,44 @@
     new_momentum[...] = fresh
     rows[mp] = total + 0.95 * fresh
 
-    def mp_copy(o):
-        return remote(rows.at[mp], rows.at[mp], mp_ss.at[o - 1], mp_rs.at[o - 1], (dp, lax.rem(mp + o, NMP)))
-
-    def mp_arrival(o):
-        other = lax.rem(mp + NMP - o, NMP)
-        return remote(rows.at[other], rows.at[other], mp_ss.at[o - 1], mp_rs.at[o - 1], (dp, lax.rem(mp + o, NMP)))
-
-    for o in range(1, NMP):
-        mp_copy(o).start()
-    for o in range(1, NMP):
-        mp_arrival(o).wait_recv()
+    x, core = mp // 2, lax.rem(mp, 2)
+    sibling = (dp, 2 * x + 1 - core)
+    piece = 64 // PIECES
+
+    def row_copy(index, owner, part, device):
+        ref = rows.at[owner, pl.ds(part * piece, piece)]
+        return remote(ref, ref, mp_ss.at[index, part], mp_rs.at[index, part], device)
+
+    def chip(o):
+        return 2 * lax.rem(x + o, 4) + core
+
+    def pair_of(owner):
+        return owner + 1 - 2 * lax.rem(owner, 2)
+
+    def to_chip(o, part):
+        return row_copy(o - 1, mp, part, (dp, chip(o)))
+
+    def from_chip(o, part):
+        return row_copy(o - 1, chip(4 - o), part, sibling)
+
+    def pass_on(o, part):
+        return row_copy(o + 3, chip(4 - o), part, sibling)
+
+    def passed(o, part):
+        return row_copy(o + 3, pair_of(chip(4 - o)), part, sibling)
+
+    for part in range(PIECES):
+        for o in (2, 1, 3):
+            to_chip(o, part).start()
+        row_copy(3, mp, part, sibling).start()
+    for part in range(PIECES):
+        for o in (1, 3, 2):
+            from_chip(o, part).wait_recv()
+            pass_on(o, part).start()
+    for part in range(PIECES):
+        row_copy(3, pair_of(mp), part, sibling).wait_recv()
+        for o in (1, 3, 2):
+            passed(o, part).wait_recv()
 
     whole = rows[...].reshape(NMP * 64, 256)
     scale = 1.0 / (jnp.sqrt(jnp.sum(whole * whole, keepdims=True)) + 1e-07)
@@ -198,27 +226,20 @@
             for c in children(SPREAD_PARENT, d):
                 if c < 8 or way == 0:
                     spread(kind, way, sign, c, 1).start()
-            if kind == "m":
+        if kind == "m":
+            for way, sign in ways(d):
                 send_across(-sign * d, len(sent))
                 sent.append((-sign * d, len(sent)))
     for dz, index in sent:
         for o in range(1, NY):
             across_arrival(o, lax.rem(z + dz + NZ, NZ), first_rows, index).wait_recv()
 
-    part = 16
-    stores = []
-    for first in range(0, NY * NZ, part):
-        def place(i, _):
-            slot = table[1, first + i]
-            ordered[first + i] = final[lax.rem(slot // NZ + NY - y, NY), lax.rem(slot, NZ)]
-            return 0
-
-        lax.fori_loop(0, part, place, 0)
-        store = pltpu.make_async_copy(
-            ordered.at[pl.ds(first, part)], updates.at[pl.ds(first, part)], out_sem.at[first // part]
-        )
-        store.start()
-        stores.append(store)
+    def place(i, _):
+        slot = table[1, i]
+        updates[i] = final[lax.rem(slot // NZ + NY - y, NY), lax.rem(slot, NZ)]
+        return 0
+
+    lax.fori_loop(0, NY * NZ, place, 0)
 
     for d in SUM_ORDER:
         for o in range(1, NY):
@@ -228,15 +249,16 @@
                 z_copy(way, sign, d).wait_send()
                 spread("m", way, sign, d, 1).wait_send()
                 spread("b", way, sign, d, 1).wait_send()
-    for o in range(1, NMP):
-        mp_copy(o).wait_send()
+    for part in range(PIECES):
+        row_copy(3, mp, part, sibling).wait_send()
+        for o in range(1, 4):
+            to_chip(o, part).wait_send()
+            pass_on(o, part).wait_send()
     for dz, index in sent:
         for o in range(1, NY):
             across(o, lax.rem(z + dz + NZ, NZ), first_rows, index).wait_send()
     for o in range(1, NY):
         across(o, z, other_rows, 16).wait_send()
-    for store in stores:
-        store.wait()
 
 
 def shards(grads, momentum, slots):
@@ -258,7 +280,7 @@
             jax.ShapeDtypeStruct((64, 256), F32),
         ),
         in_specs=[smem, anywhere, vmem],
-        out_specs=(anywhere, vmem),
+        out_specs=(vmem, vmem),
         scratch_shapes=[
             pltpu.VMEM((64, 64, 256), BF16),
             pltpu.VMEM((3, 16, 64, 256), BF16),
@@ -267,9 +289,8 @@
             pltpu.VMEM((2, 8, 64, 256), F32),
             pltpu.VMEM((NMP, 64, 256), F32),
             pltpu.VMEM((NY, NZ, 64, 256), BF16),
-            pltpu.VMEM((64, 64, 256), BF16),
-            dma, dma((3, 9)), dma((3, 9)), dma((2, 8)), dma((2, 8)), dma((7,)), dma((7,)),
-            dma((2, 2, 8)), dma((2, 2, 8)), dma((3, 17)), dma((3, 17)), dma((4,)),
+            dma, dma((3, 9)), dma((3, 9)), dma((2, 8)), dma((2, 8)), dma((7, PIECES)), dma((7, PIECES)),
+            dma((2, 2, 8)), dma((2, 2, 8)), dma((3, 17)), dma((3, 17)),
         ],
         compiler_params=pltpu.CompilerParams(
             collective_id=0, has_side_effects=True, vmem_limit_bytes=50 * 2**20

time: 85.6 us -> 84.7 us (0.989)
  Pallas kernels: 81.2 us -> 80.3 us
    pallas_call x1, Pallas kernels: 81.2 us -> 80.3 us  [shards(): pl.pallas_call(kernel, out_shape=(jax.ShapeDtypeStruct((64, 64, 256), BF1...]
where the time goes in v3:
time: 84.7 us; the launch traced here: 84.5 us
  Pallas kernels  80.3 us (95%)
  local copies, waits for them, and re-layouts  2.79 us (3%)
    pallas_call x1, Pallas kernels, shards(): pl.pallas_call(kernel, out_shape=(jax.ShapeDtypeStruct((64, 64, 256), BF1...  80.3 us
    unnamed x4, local copies, waits for them, and re-layouts  2.79 us

profile of v3, /device:TPU:1, one launch (start us, length us, event | category | flops | bytes accessed | tf_op | source)
XLA Modules:
  0.0 84.5 jit_solution(7407411680085943115)
XLA Ops:
  0.6 0.8 select_reduce_fusion.table
  1.4 0.0 copy-start
  1.4 0.8 copy-done
  2.2 80.3 %shard_map.50 = (bf16[64,64,256]{2,1,0:T(8,128)(2,1)S(1)}, f32[64,256]{1,0:T(8,128)S(1)}) custom-call(s32[2,64]{1,0:T(2,128)S(1)} %select_reduce_fusion.table, bf16[1,64,64,256]{3,2,1,0:T(8,128)(2,1)} %grads.1, f32[64,256]{1,0:T(8,128)S(1)} %bitcast.2), custom_call_target="tpu_custom_call" | custom-call | tf_op jit(solution)/shard_map/pallas_call | solution.py:276
  82.6 1.3 %copy.7 = bf16[64,64,256]{2,1,0:T(8,128)(2,1)} copy(bf16[64,64,256]{2,1,0:T(8,128)(2,1)S(1)} %get-tuple-element.8) | data formatting | bytes 4194304
  83.9 0.6 copy.8
  (1 shorter events, 0.0 us)
Async XLA Ops:
  1.4 0.8 copy-start

commit v4 on v3

--- a/solution.py
+++ b/solution.py
@@ -152,6 +152,12 @@
         for o in (2, 1, 3):
             to_chip(o, part).start()
         row_copy(3, mp, part, sibling).start()
+    for d in SUM_ORDER:
+        for o in range(1, NY):
+            y_copy(o, d).wait_send()
+        for way, sign in ways(d):
+            if d:
+                z_copy(way, sign, d).wait_send()
     for part in range(PIECES):
         for o in (1, 3, 2):
             from_chip(o, part).wait_recv()
@@ -230,35 +236,31 @@
             for way, sign in ways(d):
                 send_across(-sign * d, len(sent))
                 sent.append((-sign * d, len(sent)))
-    for dz, index in sent:
-        for o in range(1, NY):
-            across_arrival(o, lax.rem(z + dz + NZ, NZ), first_rows, index).wait_recv()
-
-    def place(i, _):
-        slot = table[1, i]
-        updates[i] = final[lax.rem(slot // NZ + NY - y, NY), lax.rem(slot, NZ)]
-        return 0
-
-    lax.fori_loop(0, NY * NZ, place, 0)
-
-    for d in SUM_ORDER:
-        for o in range(1, NY):
-            y_copy(o, d).wait_send()
-        for way, sign in ways(d):
-            if d:
-                z_copy(way, sign, d).wait_send()
-                spread("m", way, sign, d, 1).wait_send()
-                spread("b", way, sign, d, 1).wait_send()
     for part in range(PIECES):
         row_copy(3, mp, part, sibling).wait_send()
         for o in range(1, 4):
             to_chip(o, part).wait_send()
             pass_on(o, part).wait_send()
+    for d in SUM_ORDER:
+        for way, sign in ways(d):
+            if d:
+                spread("m", way, sign, d, 1).wait_send()
+                spread("b", way, sign, d, 1).wait_send()
     for dz, index in sent:
         for o in range(1, NY):
             across(o, lax.rem(z + dz + NZ, NZ), first_rows, index).wait_send()
     for o in range(1, NY):
         across(o, z, other_rows, 16).wait_send()
+    for dz, index in sent:
+        for o in range(1, NY):
+            across_arrival(o, lax.rem(z + dz + NZ, NZ), first_rows, index).wait_recv()
+
+    def place(i, _):
+        slot = table[1, i]
+        updates[i] = final[lax.rem(slot // NZ + NY - y, NY), lax.rem(slot, NZ)]
+        return 0
+
+    lax.fori_loop(0, NY * NZ, place, 0)
 
 
 def shards(grads, momentum, slots):

time: 84.7 us -> 84.5 us (level)
  no operation moved by 1% of the time
where the time goes in v4:
time: 84.5 us; the launch traced here: 84.3 us
  Pallas kernels  80.1 us (95%)
  local copies, waits for them, and re-layouts  2.79 us (3%)
    pallas_call x1, Pallas kernels, shards(): pl.pallas_call(kernel, out_shape=(jax.ShapeDtypeStruct((64, 64, 256), BF1...  80.1 us
    unnamed x4, local copies, waits for them, and re-layouts  2.79 us

profile of v4, /device:TPU:1, one launch (start us, length us, event | category | flops | bytes accessed | tf_op | source)
XLA Modules:
  0.0 84.3 jit_solution(14027779965367995183)
XLA Ops:
  0.6 0.8 select_reduce_fusion.table
  1.4 0.0 copy-start
  1.4 0.8 copy-done
  2.2 80.1 %shard_map.50 = (bf16[64,64,256]{2,1,0:T(8,128)(2,1)S(1)}, f32[64,256]{1,0:T(8,128)S(1)}) custom-call(s32[2,64]{1,0:T(2,128)S(1)} %select_reduce_fusion.table, bf16[1,64,64,256]{3,2,1,0:T(8,128)(2,1)} %grads.1, f32[64,256]{1,0:T(8,128)S(1)} %bitcast.2), custom_call_target="tpu_custom_call" | custom-call | tf_op jit(solution)/shard_map/pallas_call | solution.py:278
  82.4 1.3 %copy.7 = bf16[64,64,256]{2,1,0:T(8,128)(2,1)} copy(bf16[64,64,256]{2,1,0:T(8,128)(2,1)S(1)} %get-tuple-element.8) | data formatting | bytes 4194304
  83.7 0.6 copy.8
  (1 shorter events, 0.0 us)
Async XLA Ops:
  1.4 0.8 copy-start
